TPU v7x, 128 devices: a whole 4x4x4 slice. The times are simulated.
128 devices in a mesh: dp: 4 (over y), pipe: 4 (over z), expert: 8 (over x, core).
Axes of the slice: x: 4, y: 4, z: 4, core: 2. Of those that a mesh axis runs over, the one named last changes fastest.
Arguments:
- tokens: bfloat16 [4, 4096, 5120], P('pipe', ('dp', 'expert')), may hold values from -6 to 6
- cotangent: bfloat16 [4, 4096, 5120], P('pipe', ('dp', 'expert')), may hold values from -6 to 6
- gain: float32 [4, 5120], P('pipe'), may hold values from 0.1 to 1.9
- w_gate: bfloat16 [4, 8, 5120, 768], P('pipe', 'expert', 'dp'), may hold values from -0.078125 to 0.078125
- w_up: bfloat16 [4, 8, 5120, 768], P('pipe', 'expert', 'dp'), may hold values from -0.078125 to 0.078125
- w_down: bfloat16 [4, 8, 768, 5120], P('pipe', 'expert', None, 'dp'), may hold values from -0.21875 to 0.21875
- route: int32 [4, 4, 512, 1], P('pipe', None, ('dp', 'expert')), may hold values from 0 to 7; in each aligned block of 16 rows (0 to 15, 16 to 31, ..., all dimensions but the last counted through in order) at most 3 rows name the same one
Outputs:
- out_tokens: bfloat16 [4, 4096, 5120], P('pipe', ('dp', 'expert'))
- grad_tokens: bfloat16 [4, 4096, 5120], P('pipe', ('dp', 'expert'))
- grad_gain: float32 [4, 5120], P('pipe')
- grad_gate: bfloat16 [4, 8, 5120, 768], P('pipe', 'expert', 'dp')
- grad_up: bfloat16 [4, 8, 5120, 768], P('pipe', 'expert', 'dp')
- grad_down: bfloat16 [4, 8, 768, 5120], P('pipe', 'expert', None, 'dp')
Inputs may be any that keep to these rules, and one draw needn't show every extreme that they name: route[l, m, t, 0] is the expert of tile t at layer l for micro-batch m. Among the 16 tiles of one device for one layer and one micro-batch (aligned blocks), no expert is named more than 3 times; every expert is named somewhere.
All inputs are finite; a program needn't handle non-finite values.
Results may differ from a plain program's by a relative error of at most 0.034.
Values may be sent and summed in bfloat16 or wider, within the bound.
A program may use at most 128 MiB of HBM per device.

v0:
```python
import jax
import jax.numpy as jnp
from jax import lax
from jax.sharding import PartitionSpec as P

TILE = 8
PASSES = 2
epsilon = 1e-06


def shifted(block, axis, distance):
    devices = range(lax.axis_size(axis))
    route = [((i - distance) % len(devices), i) for i in devices]
    return lax.ppermute(block, axis, route)


def contract_last(former, latter):
    return lax.dot_general(
        former, latter, (((1,), (1,)), ((), ())), preferred_element_type=jnp.float32
    )


def contract_first(former, latter):
    return lax.dot_general(
        former, latter, (((0,), (0,)), ((), ())), preferred_element_type=jnp.float32
    )


def normalize(hidden, gain_row):
    widened = hidden.astype(jnp.float32)
    inverse = lax.rsqrt(jnp.mean(widened * widened, axis=-1, keepdims=True) + epsilon)
    scaled = widened * inverse
    return ((scaled * gain_row).astype(jnp.bfloat16), scaled, inverse)


def slot_matrix(route_now, expert_count, capacity):
    tile_count = route_now.shape[0]
    expert_ids = jnp.arange(expert_count, dtype=jnp.int32)
    member = (route_now[None, :] == expert_ids[:, None]).astype(jnp.int32)
    earlier = jnp.cumsum(member, axis=1) - member
    rank_ids = jnp.arange(capacity, dtype=jnp.int32)
    placed = member[:, None, :] * (earlier[:, None, :] == rank_ids[None, :, None]).astype(jnp.int32)
    return placed.reshape(expert_count * capacity, tile_count)


def into_slots(placed, rows, tile_rows, dp_count):
    width = rows.shape[-1]
    tile_blocks = rows.reshape(placed.shape[1], tile_rows, dp_count, width // dp_count)
    return jnp.einsum(
        "st,trqd->qsrd",
        placed.astype(jnp.bfloat16),
        tile_blocks,
        preferred_element_type=jnp.float32,
    ).astype(jnp.bfloat16)


def from_slots(placed, slot_rows):
    merged = jnp.einsum(
        "st,qsrd->trqd", placed.astype(jnp.bfloat16), slot_rows, preferred_element_type=jnp.float32
    ).astype(jnp.bfloat16)
    return merged.reshape(merged.shape[0] * merged.shape[1], -1)


def send_out(slot_rows):
    quarter = slot_rows.shape[-1]
    flat = slot_rows.reshape((-1,) + slot_rows.shape[2:])
    arrived = lax.all_to_all(flat, ("dp", "expert"), split_axis=0, concat_axis=0, tiled=True)
    return arrived.reshape(-1, quarter)


def send_back(part_rows, dp_count, tile_rows):
    quarter = part_rows.shape[-1]
    flat = part_rows.reshape(-1, tile_rows, quarter)
    returned = lax.all_to_all(flat, ("dp", "expert"), split_axis=0, concat_axis=0, tiled=True)
    return returned.reshape(dp_count, -1, tile_rows, quarter)


def widen_rounded(values):
    return lax.optimization_barrier(values.astype(jnp.bfloat16)).astype(jnp.float32)


def expert_forward(received, gate_weight, up_weight, down_weight):
    gate_terms = widen_rounded(jnp.dot(received, gate_weight, preferred_element_type=jnp.float32))
    up_terms = widen_rounded(jnp.dot(received, up_weight, preferred_element_type=jnp.float32))
    gate_pre, up_pre = (
        lax.psum(gate_terms.astype(jnp.bfloat16), "dp").astype(jnp.float32),
        lax.psum(up_terms.astype(jnp.bfloat16), "dp").astype(jnp.float32),
    )
    activated = (jax.nn.silu(gate_pre) * up_pre).astype(jnp.bfloat16)
    part_rows = jnp.dot(activated, down_weight, preferred_element_type=jnp.float32).astype(
        jnp.bfloat16
    )
    return (part_rows, (gate_pre, up_pre, activated))


def expert_backward(
    received, grad_recv, kept_state, gate_weight, up_weight, down_weight, grad_sums
):
    gate_pre, up_pre, activated = kept_state
    grad_terms = widen_rounded(contract_last(grad_recv, down_weight))
    grad_act = lax.psum(grad_terms.astype(jnp.bfloat16), "dp").astype(jnp.float32)
    sigmoid_gate = jax.nn.sigmoid(gate_pre)
    silu_gate = gate_pre * sigmoid_gate
    grad_gate_pre = (
        grad_act * up_pre * sigmoid_gate * (1.0 + gate_pre * (1.0 - sigmoid_gate))
    ).astype(jnp.bfloat16)
    grad_up_pre = (grad_act * silu_gate).astype(jnp.bfloat16)
    back_rows = (
        contract_last(grad_gate_pre, gate_weight) + contract_last(grad_up_pre, up_weight)
    ).astype(jnp.bfloat16)
    grad_gate = grad_sums[0] + contract_first(received, grad_gate_pre)
    grad_up = grad_sums[1] + contract_first(received, grad_up_pre)
    grad_down = grad_sums[2] + contract_first(activated, grad_recv)
    return (back_rows, (grad_gate, grad_up, grad_down))


def body(tokens, cotangent, gain, w_gate, w_up, w_down, route):
    pipe_count = lax.axis_size("pipe")
    dp_count = lax.axis_size("dp")
    expert_count = lax.axis_size("expert")
    section_index = lax.axis_index("pipe")
    gain_row = gain[0]
    gate_weight = w_gate[0, 0]
    up_weight = w_up[0, 0]
    down_weight = w_down[0, 0]
    route_table = route[0, :, :, 0]
    tile_count = route_table.shape[1]
    capacity = max(2, 3 * tile_count // (2 * expert_count))
    hidden = tokens[0]
    saved_ticks = []
    out_rows = hidden
    for pass_index in range(PASSES):
        micro_index = (section_index - pass_index + pipe_count) % pipe_count
        route_now = lax.dynamic_index_in_dim(route_table, micro_index, 0, keepdims=False)
        placed = slot_matrix(route_now, expert_count, capacity)
        normed, scaled, inverse = normalize(hidden, gain_row)
        received = send_out(into_slots(placed, normed, TILE, dp_count))
        part_rows, kept_state = expert_forward(received, gate_weight, up_weight, down_weight)
        ffn_rows = from_slots(placed, send_back(part_rows, dp_count, TILE))
        new_hidden = (hidden.astype(jnp.float32) + ffn_rows.astype(jnp.float32)).astype(
            jnp.bfloat16
        )
        saved_ticks.append((placed, scaled, inverse, received, kept_state))
        if pass_index + 1 < PASSES:
            hidden = shifted(new_hidden, "pipe", 1)
        else:
            out_rows = new_hidden
    grad_rows = cotangent[0]
    grad_sums = (
        jnp.zeros(gate_weight.shape, jnp.float32),
        jnp.zeros(up_weight.shape, jnp.float32),
        jnp.zeros(down_weight.shape, jnp.float32),
    )
    gain_sum = jnp.zeros(gain_row.shape, jnp.float32)
    entry_grad = grad_rows
    for pass_index in reversed(range(PASSES)):
        placed, scaled, inverse, received, kept_state = saved_ticks[pass_index]
        grad_recv = send_out(into_slots(placed, grad_rows, TILE, dp_count))
        back_rows, grad_sums = expert_backward(
            received, grad_recv, kept_state, gate_weight, up_weight, down_weight, grad_sums
        )
        grad_normed = from_slots(placed, send_back(back_rows, dp_count, TILE)).astype(jnp.float32)
        gain_sum = gain_sum + jnp.sum(grad_normed * scaled, axis=0)
        grad_scaled = grad_normed * gain_row
        grad_wide = inverse * (
            grad_scaled - scaled * jnp.mean(grad_scaled * scaled, axis=-1, keepdims=True)
        )
        grad_in = (grad_rows.astype(jnp.float32) + grad_wide).astype(jnp.bfloat16)
        if pass_index > 0:
            grad_rows = shifted(grad_in, "pipe", -1)
        else:
            entry_grad = grad_in
    gain_total = lax.psum(gain_sum, ("dp", "expert"))
    return (
        out_rows[None],
        entry_grad[None],
        gain_total[None],
        grad_sums[0].astype(jnp.bfloat16)[None, None],
        grad_sums[1].astype(jnp.bfloat16)[None, None],
        grad_sums[2].astype(jnp.bfloat16)[None, None],
    )


def solution(mesh):
    placed = (
        P("pipe", ("dp", "expert"), None),
        P("pipe", ("dp", "expert"), None),
        P("pipe", None),
        P("pipe", "expert", "dp", None),
        P("pipe", "expert", "dp", None),
        P("pipe", "expert", None, "dp"),
        P("pipe", None, ("dp", "expert"), None),
    )
    return jax.shard_map(
        body,
        mesh=mesh,
        in_specs=placed,
        out_specs=(
            P("pipe", ("dp", "expert"), None),
            P("pipe", ("dp", "expert"), None),
            P("pipe", None),
            P("pipe", "expert", "dp", None),
            P("pipe", "expert", "dp", None),
            P("pipe", "expert", None, "dp"),
        ),
        check_vma=False,
    )
```

profile of v0, /device:TPU:0, one launch (start us, length us, event | category | flops | bytes accessed | tf_op | source)
XLA Modules:
  0.0 713.0 jit_solution(6603323839218652019)
XLA Ops:
  8.4 1.6 fusion.28
  10.0 1.1 fusion.36
  13.2 34.5 %all_to_all.40 = bf16[96,8,1280]{2,1,0:T(8,128)(2,1)S(1)} all-to-all(bf16[96,8,1280]{2,1,0:T(8,128)(2,1)S(1)} %copy.49), channel_id=1, replica_groups=mesh['dp'=4,'pipe'=4,'expert'=8] {'dp','expert'}, dimensions={0} | all-to-all | bytes 3932160 | tf_op jit(solution)/shard_map/all_to_all | solution.py:67
  47.7 2.7 fusion.94
  50.4 2.7 fusion.99
  53.2 62.0 %all-reduce.10.cloned.1.call-done = (bf16[768,768]{1,0:T(8,128)(2,1)}, bf16[768,768]{1,0:T(8,128)(2,1)}) async-done(((bf16[768,768]{1,0:T(8,128)(2,1)}, bf16[768,768]{1,0:T(8,128)(2,1)}), (bf16[768,768]{1,0:T(8,128)(2,1)}, bf16[768,768]{1,0:T(8,128)(2,1)})) %all-reduce.10.cloned.1.call-update) | async-done | bytes 2359312 | tf_op jit(solution)/shard_map/psum | solution.py:87
  115.2 3.8 fusion.12
  118.9 32.6 %all_to_all.41 = bf16[96,8,1280]{2,1,0:T(8,128)(2,1)S(1)} all-to-all(bf16[96,8,1280]{2,1,0:T(8,128)(2,1)S(1)} %fusion.12), channel_id=1, replica_groups=mesh['dp'=4,'pipe'=4,'expert'=8] {'dp','expert'}, dimensions={0} | all-to-all | bytes 3932160 | tf_op jit(solution)/shard_map/all_to_all | solution.py:74
  152.1 1.7 copy.124
  154.2 1.4 fusion.29
  155.6 2.0 collective-permute-start
  157.8 2.9 convolution_convert_fusion.1
  160.7 2.4 copy.61
  163.1 4.9 all-to-all-start.4
  167.9 20.4 %collective-permute-done = bf16[128,5120]{1,0:T(8,128)(2,1)} collective-permute-done((bf16[128,5120]{1,0:T(8,128)(2,1)}, bf16[128,5120]{1,0:T(8,128)(2,1)}, u32[]{:S(2)}, u32[]{:S(2)}) %collective-permute-start) | collective-permute-done | bytes 1310752 | tf_op jit(solution)/shard_map/ppermute | solution.py:14
  188.4 1.7 fusion.26
  190.0 1.7 fusion.19
  192.7 2.4 copy.55
  195.1 1.3 all-to-all-done.4
  196.4 4.7 all-to-all-start.2
  201.2 4.3 fusion.114
  205.4 24.1 %all-to-all-done.2 = bf16[96,8,1280]{2,1,0:T(8,128)(2,1)} async-done(((bf16[96,8,1280]{2,1,0:T(8,128)(2,1)}), bf16[96,8,1280]{2,1,0:T(8,128)(2,1)}, u32[]{:S(2)}, u32[]{:S(2)}) %all-to-all-start.2) | async-done | bytes 1966112 | tf_op jit(solution)/shard_map/all_to_all | solution.py:67
  229.5 5.0 fusion.104
  234.5 4.3 fusion.109
  238.8 79.5 %all-reduce.8.cloned.1.call-done = (bf16[768,768]{1,0:T(8,128)(2,1)}, bf16[768,768]{1,0:T(8,128)(2,1)}, bf16[768,768]{1,0:T(8,128)(2,1)}) async-done(((bf16[768,768]{1,0:T(8,128)(2,1)}, bf16[768,768]{1,0:T(8,128)(2,1)}, bf16[768,768]{1,0:T(8,128)(2,1)}), (bf16[768,768]{1,0:T(8,128)(2,1)}, bf16[768,768]{1,0:T(8,128)(2,1)}, bf16[768,768]{1,0:T(8,128)(2,1)})) %all-reduce.8.cloned.1.call-update) | async-done | bytes 3538960 | tf_op jit(solution)/shard_map/psum | solution.py:87
  318.3 5.0 fusion.13
  323.4 5.9 all-to-all-start.3
  329.3 5.3 fusion.81
  334.6 3.5 fusion.14
  338.1 19.6 %all-to-all-done.3 = bf16[96,8,1280]{2,1,0:T(8,128)(2,1)} async-done(((bf16[96,8,1280]{2,1,0:T(8,128)(2,1)}), bf16[96,8,1280]{2,1,0:T(8,128)(2,1)}, u32[]{:S(2)}, u32[]{:S(2)}) %all-to-all-start.3) | async-done | bytes 1966112 | tf_op jit(solution)/shard_map/all_to_all | solution.py:74
  357.7 4.7 all-to-all-start.5
  362.5 2.1 fusion.9
  364.6 1.7 copy.123
  366.3 1.9 copy.91
  368.2 22.7 %all-to-all-done.5 = bf16[96,8,1280]{2,1,0:T(8,128)(2,1)} async-done(((bf16[96,8,1280]{2,1,0:T(8,128)(2,1)}), bf16[96,8,1280]{2,1,0:T(8,128)(2,1)}, u32[]{:S(2)}, u32[]{:S(2)}) %all-to-all-start.5) | async-done | bytes 1966112 | tf_op jit(solution)/shard_map/all_to_all | solution.py:74
  390.9 2.1 fusion.7
  393.0 1.7 copy.122
  395.2 2.5 fusion.25
  397.6 3.5 fusion.24
  401.2 2.9 collective-permute-start.1
  404.1 26.3 %collective-permute-done.1 = bf16[128,5120]{1,0:T(8,128)(2,1)} collective-permute-done((bf16[128,5120]{1,0:T(8,128)(2,1)S(1)}, bf16[128,5120]{1,0:T(8,128)(2,1)}, u32[]{:S(2)}, u32[]{:S(2)}) %collective-permute-start.1) | collective-permute-done | bytes 1310752 | tf_op jit(solution)/shard_map/ppermute | solution.py:14
  430.4 3.7 reshape.517
  434.1 2.3 convolution_convert_fusion
  436.4 2.4 copy.67
  438.7 5.3 all-to-all-start.6
  444.6 2.4 reshape.528
  448.3 5.9 fusion.62
  454.2 18.3 %all-to-all-done.6 = bf16[96,8,1280]{2,1,0:T(8,128)(2,1)} async-done(((bf16[96,8,1280]{2,1,0:T(8,128)(2,1)}), bf16[96,8,1280]{2,1,0:T(8,128)(2,1)}, u32[]{:S(2)}, u32[]{:S(2)}) %all-to-all-start.6) | async-done | bytes 1966112 | tf_op jit(solution)/shard_map/all_to_all | solution.py:67
  472.5 4.3 fusion.119
  476.8 6.1 fusion.58
  482.9 5.5 fusion.64
  488.4 33.1 %all-reduce.6.cloned.1.call-done = bf16[768,768]{1,0:T(8,128)(2,1)} async-done(((bf16[768,768]{1,0:T(8,128)(2,1)}), bf16[768,768]{1,0:T(8,128)(2,1)}) %all-reduce.6.cloned.1.call-update) | async-done | bytes 1179664 | tf_op jit(solution)/shard_map/psum | solution.py:101
  521.5 5.3 fusion.79
  526.8 3.5 fusion.15
  530.4 6.8 all-to-all-start.7
  537.3 6.7 fusion.18
  544.0 3.2 fusion.17
  547.2 3.3 fusion.16
  550.5 15.1 %all-to-all-done.7 = bf16[96,8,1280]{2,1,0:T(8,128)(2,1)} async-done(((bf16[96,8,1280]{2,1,0:T(8,128)(2,1)}), bf16[96,8,1280]{2,1,0:T(8,128)(2,1)}, u32[]{:S(2)}, u32[]{:S(2)}) %all-to-all-start.7) | async-done | bytes 1966112 | tf_op jit(solution)/shard_map/all_to_all | solution.py:74
  565.6 5.9 multiply_reduce_fusion
  571.5 125.2 %psum.55 = f32[1,5120]{1,0:T(1,128)} all-reduce(f32[1,5120]{1,0:T(1,128)S(1)} %bitcast.217), channel_id=1, replica_groups=mesh['dp'=4,'pipe'=4,'expert'=8] {'dp','expert'}, use_global_device_ids=true, to_apply=%region_14.15 | all-reduce | flops 5120 | bytes 40960 | tf_op jit(solution)/shard_map/psum | solution.py:173
  696.7 3.4 copy.121
  700.2 2.0 copy.93
  702.3 4.0 fusion.124
  (83 shorter events, 8.1 us)
Async XLA Ops:
  7.2 108.0 %copy-start = (bf16[1,1,768,1280]{3,2,1,0:T(8,128)(2,1)S(1)}, bf16[1,1,768,1280]{3,2,1,0:T(8,128)(2,1)}, u32[]{:S(2)}) copy-start(bf16[1,1,768,1280]{3,2,1,0:T(8,128)(2,1)} %param.12) | copy-start | bytes 5898244
  7.2 2.8 copy-start.1
  7.2 108.0 %all-reduce.10.cloned.1.call-start = ((), (), s32[]{:S(2)}) async-start(), calls=%async_computation.10 | async-start | bytes 4718592 | tf_op jit(solution)/shard_map/psum | solution.py:87
  13.2 34.5 %copy-start.7 = (bf16[1,1,1280,768]{3,2,1,0:T(8,128)(2,1)S(1)}, bf16[1,1,1280,768]{3,2,1,0:T(8,128)(2,1)}, u32[]{:S(2)}) copy-start(bf16[1,1,1280,768]{3,2,1,0:T(8,128)(2,1)} %param.10) | copy-start | bytes 5898244
  47.7 2.7 copy-start.4
  47.7 2.7 copy-start.8
  155.6 32.8 %collective-permute-start = (bf16[128,5120]{1,0:T(8,128)(2,1)}, bf16[128,5120]{1,0:T(8,128)(2,1)}, u32[]{:S(2)}, u32[]{:S(2)}) collective-permute-start(bf16[128,5120]{1,0:T(8,128)(2,1)} %fusion.29), channel_id=1, source_target_pairs={{24,0},{0,8},{8,16},{16,24},{25,1},{1,9},{9,17},{17,25},{26,2},{2,... | collective-permute-start | bytes 3932168 | tf_op jit(solution)/shard_map/ppermute | solution.py:14
  163.1 27.0 %copy-start.6 = (f32[1,5120]{1,0:T(1,128)S(1)}, f32[1,5120]{1,0:T(1,128)}, u32[]{:S(2)}) copy-start(f32[1,5120]{1,0:T(1,128)} %param.9) | copy-start | bytes 61444
  163.1 33.3 %all-to-all-start.4 = ((bf16[96,8,1280]{2,1,0:T(8,128)(2,1)}), bf16[96,8,1280]{2,1,0:T(8,128)(2,1)}, u32[]{:S(2)}, u32[]{:S(2)}) async-start(bf16[96,8,1280]{2,1,0:T(8,128)(2,1)} %copy.61), calls=%async_computation.4 | async-start | bytes 3932160 | tf_op jit(solution)/shard_map/all_to_all | solution.py:67
  196.4 33.2 %all-to-all-start.2 = ((bf16[96,8,1280]{2,1,0:T(8,128)(2,1)}), bf16[96,8,1280]{2,1,0:T(8,128)(2,1)}, u32[]{:S(2)}, u32[]{:S(2)}) async-start(bf16[96,8,1280]{2,1,0:T(8,128)(2,1)} %copy.55), calls=%async_computation.2 | async-start | bytes 3932160 | tf_op jit(solution)/shard_map/all_to_all | solution.py:67
  201.1 117.2 %all-reduce.8.cloned.1.call-start = ((), (), s32[]{:S(2)}) async-start(), calls=%async_computation.9 | async-start | bytes 7077888 | tf_op jit(solution)/shard_map/psum | solution.py:87
  229.5 5.0 copy-start.9
  323.4 34.3 %all-to-all-start.3 = ((bf16[96,8,1280]{2,1,0:T(8,128)(2,1)}), bf16[96,8,1280]{2,1,0:T(8,128)(2,1)}, u32[]{:S(2)}, u32[]{:S(2)}) async-start(bf16[96,8,1280]{2,1,0:T(8,128)(2,1)} %fusion.13), calls=%async_computation.3 | async-start | bytes 3932160 | tf_op jit(solution)/shard_map/all_to_all | solution.py:74
  329.3 5.3 copy-start.10
  329.3 5.3 copy-start.16
  329.3 5.3 copy-start.18
  357.7 33.2 %all-to-all-start.5 = ((bf16[96,8,1280]{2,1,0:T(8,128)(2,1)}), bf16[96,8,1280]{2,1,0:T(8,128)(2,1)}, u32[]{:S(2)}, u32[]{:S(2)}) async-start(bf16[96,8,1280]{2,1,0:T(8,128)(2,1)} %fusion.14), calls=%async_computation.5 | async-start | bytes 3932160 | tf_op jit(solution)/shard_map/all_to_all | solution.py:74
  395.1 2.5 copy-start.2
  395.1 2.5 copy-start.3
  401.2 29.2 %collective-permute-start.1 = (bf16[128,5120]{1,0:T(8,128)(2,1)S(1)}, bf16[128,5120]{1,0:T(8,128)(2,1)}, u32[]{:S(2)}, u32[]{:S(2)}) collective-permute-start(bf16[128,5120]{1,0:T(8,128)(2,1)S(1)} %get-tuple-element.15), channel_id=1, source_target_pairs={{8,0},{16,8},{24,16},{0,24},{9,1},{17,9},{25,17},{1,25},{10,2},{18... | collective-permute-start | bytes 3932168 | tf_op jit(solution)/shard_map/ppermute | solution.py:14
  438.7 33.7 %all-to-all-start.6 = ((bf16[96,8,1280]{2,1,0:T(8,128)(2,1)}), bf16[96,8,1280]{2,1,0:T(8,128)(2,1)}, u32[]{:S(2)}, u32[]{:S(2)}) async-start(bf16[96,8,1280]{2,1,0:T(8,128)(2,1)} %copy.67), calls=%async_computation.6 | async-start | bytes 3932160 | tf_op jit(solution)/shard_map/all_to_all | solution.py:67
  444.0 77.5 %all-reduce.6.cloned.1.call-start = ((), (), s32[]{:S(2)}) async-start(), calls=%async_computation.8 | async-start | bytes 2359296 | tf_op jit(solution)/shard_map/psum | solution.py:101
  476.8 6.2 copy-start.15
  476.8 6.1 copy-start.17
  476.8 6.1 copy-start.19
  521.5 5.3 copy-start.11
  521.5 5.3 copy-start.13
  521.5 5.3 copy-start.20
  530.4 35.3 %all-to-all-start.7 = ((bf16[96,8,1280]{2,1,0:T(8,128)(2,1)}), bf16[96,8,1280]{2,1,0:T(8,128)(2,1)}, u32[]{:S(2)}, u32[]{:S(2)}) async-start(bf16[96,8,1280]{2,1,0:T(8,128)(2,1)} %fusion.15), calls=%async_computation.7 | async-start | bytes 3932160 | tf_op jit(solution)/shard_map/all_to_all | solution.py:74
  537.2 6.8 copy-start.5
  537.2 6.8 copy-start.14
  537.2 6.8 copy-start.21
  537.2 6.8 copy-start.22
  544.0 3.2 copy-start.12
  544.0 3.2 copy-start.23
Sparse Core Ops, SparseCore 0:
  53.3 61.8 all-reduce.9
  238.9 79.3 all-reduce.7
  476.9 44.5 all-reduce.5
where the time goes:
time: 723 us; the launch traced here: 713 us
  waiting for transfers between devices  322 us (45%)
  blocking collectives  192 us (27%)
  matrix products  98 us (14%)
  starting transfers between devices  37.9 us (5%)
  local copies, waits for them, and re-layouts  29.4 us (4%)
  other arithmetic  18.6 us (3%)
  between operations  14.4 us (2%)
    psum x2, waiting for transfers between devices, expert_forward(): lax.psum(up_terms.astype(jnp.bfloat16), 'dp').astype(jnp.float32)  142 us
    psum x1, blocking collectives, body(): gain_total = lax.psum(gain_sum, ('dp', 'expert'))  125 us
    all_to_all x3, waiting for transfers between devices, send_back(): lax.all_to_all(flat, ('dp', 'expert'), split_axis=0, concat_axis=0, tiled...  57.4 us
    ppermute x2, waiting for transfers between devices, shifted(): return lax.ppermute(block, axis, route)  46.7 us
    all_to_all x3, waiting for transfers between devices, send_out(): lax.all_to_all(flat, ('dp', 'expert'), split_axis=0, concat_axis=0, tiled...  43.6 us
    all_to_all x1, blocking collectives, send_out(): lax.all_to_all(flat, ('dp', 'expert'), split_axis=0, concat_axis=0, tiled...  34.5 us
    psum x1, waiting for transfers between devices, expert_backward(): lax.psum(grad_terms.astype(jnp.bfloat16), 'dp').astype(jnp.float32)  33.1 us
    all_to_all x1, blocking collectives, send_back(): lax.all_to_all(flat, ('dp', 'expert'), split_axis=0, concat_axis=0, tiled...  32.6 us
  transfers between devices with their start and end apart: 11, of which 11 were waited for; matrix products, arithmetic and copies ran while one was open for 9% of the time, Pallas kernels for 0%

commit v1 on v0

--- a/solution.py
+++ b/solution.py
@@ -170,7 +170,7 @@
             grad_rows = shifted(grad_in, "pipe", -1)
         else:
             entry_grad = grad_in
-    gain_total = lax.psum(gain_sum, ("dp", "expert"))
+    gain_total = lax.psum(lax.psum(gain_sum, "dp"), "expert")
     return (
         out_rows[None],
         entry_grad[None],

time: 723 us -> 636 us (0.88)
  blocking collectives: 192 us -> 106 us
    psum x1 -> x2, blocking collectives: 125 us -> 38.9 us  [body(): gain_total = lax.psum(lax.psum(gain_sum, 'dp'), 'expert')]
  transfers between devices with their start and end apart: 11 -> 11, of which waited for: 11 -> 11; matrix products, arithmetic and copies ran while one was open for 9% -> 10% of each run, Pallas kernels for 0% -> 0%
where the time goes in v1:
time: 636 us; the launch traced here: 627 us
  waiting for transfers between devices  322 us (51%)
  blocking collectives  106 us (17%)
  matrix products  98 us (15%)
  starting transfers between devices  38 us (6%)
  local copies, waits for them, and re-layouts  29.4 us (5%)
  other arithmetic  18.6 us (3%)
  between operations  14.5 us (2%)
    psum x2, waiting for transfers between devices, expert_forward(): lax.psum(up_terms.astype(jnp.bfloat16), 'dp').astype(jnp.float32)  142 us
    all_to_all x3, waiting for transfers between devices, send_back(): lax.all_to_all(flat, ('dp', 'expert'), split_axis=0, concat_axis=0, tiled...  57.5 us
    ppermute x2, waiting for transfers between devices, shifted(): return lax.ppermute(block, axis, route)  46.7 us
    all_to_all x3, waiting for transfers between devices, send_out(): lax.all_to_all(flat, ('dp', 'expert'), split_axis=0, concat_axis=0, tiled...  43.6 us
    psum x2, blocking collectives, body(): gain_total = lax.psum(lax.psum(gain_sum, 'dp'), 'expert')  38.9 us
    all_to_all x1, blocking collectives, send_out(): lax.all_to_all(flat, ('dp', 'expert'), split_axis=0, concat_axis=0, tiled...  34.5 us
    psum x1, waiting for transfers between devices, expert_backward(): lax.psum(grad_terms.astype(jnp.bfloat16), 'dp').astype(jnp.float32)  33.1 us
    all_to_all x1, blocking collectives, send_back(): lax.all_to_all(flat, ('dp', 'expert'), split_axis=0, concat_axis=0, tiled...  32.6 us
  transfers between devices with their start and end apart: 11, of which 11 were waited for; matrix products, arithmetic and copies ran while one was open for 10% of the time, Pallas kernels for 0%

profile of v1, /device:TPU:0, one launch (start us, length us, event | category | flops | bytes accessed | tf_op | source)
XLA Modules:
  0.0 626.9 jit_solution(8641514805546403943)
XLA Ops:
  8.4 1.6 fusion.28
  13.2 34.5 %all_to_all.40 = bf16[96,8,1280]{2,1,0:T(8,128)(2,1)S(1)} all-to-all(bf16[96,8,1280]{2,1,0:T(8,128)(2,1)S(1)} %copy.49), channel_id=1, replica_groups=mesh['dp'=4,'pipe'=4,'expert'=8] {'dp','expert'}, dimensions={0} | all-to-all | bytes 3932160 | tf_op jit(solution)/shard_map/all_to_all | solution.py:67
  47.7 2.7 fusion.94
  50.4 2.7 fusion.99
  53.2 62.0 %all-reduce.10.cloned.1.call-done = (bf16[768,768]{1,0:T(8,128)(2,1)}, bf16[768,768]{1,0:T(8,128)(2,1)}) async-done(((bf16[768,768]{1,0:T(8,128)(2,1)}, bf16[768,768]{1,0:T(8,128)(2,1)}), (bf16[768,768]{1,0:T(8,128)(2,1)}, bf16[768,768]{1,0:T(8,128)(2,1)})) %all-reduce.10.cloned.1.call-update) | async-done | bytes 2359312 | tf_op jit(solution)/shard_map/psum | solution.py:87
  115.2 3.8 fusion.12
  118.9 32.6 %all_to_all.41 = bf16[96,8,1280]{2,1,0:T(8,128)(2,1)S(1)} all-to-all(bf16[96,8,1280]{2,1,0:T(8,128)(2,1)S(1)} %fusion.12), channel_id=1, replica_groups=mesh['dp'=4,'pipe'=4,'expert'=8] {'dp','expert'}, dimensions={0} | all-to-all | bytes 3932160 | tf_op jit(solution)/shard_map/all_to_all | solution.py:74
  152.1 1.7 copy.124
  154.2 1.4 fusion.29
  155.6 2.1 collective-permute-start
  157.9 2.9 convolution_convert_fusion.1
  160.8 2.4 copy.61
  163.1 4.9 all-to-all-start.4
  168.0 20.4 %collective-permute-done = bf16[128,5120]{1,0:T(8,128)(2,1)} collective-permute-done((bf16[128,5120]{1,0:T(8,128)(2,1)}, bf16[128,5120]{1,0:T(8,128)(2,1)}, u32[]{:S(2)}, u32[]{:S(2)}) %collective-permute-start) | collective-permute-done | bytes 1310752 | tf_op jit(solution)/shard_map/ppermute | solution.py:14
  188.4 1.7 fusion.26
  190.1 1.7 fusion.19
  192.8 2.4 copy.55
  195.1 1.3 all-to-all-done.4
  196.4 4.7 all-to-all-start.2
  201.2 4.3 fusion.114
  205.5 24.1 %all-to-all-done.2 = bf16[96,8,1280]{2,1,0:T(8,128)(2,1)} async-done(((bf16[96,8,1280]{2,1,0:T(8,128)(2,1)}), bf16[96,8,1280]{2,1,0:T(8,128)(2,1)}, u32[]{:S(2)}, u32[]{:S(2)}) %all-to-all-start.2) | async-done | bytes 1966112 | tf_op jit(solution)/shard_map/all_to_all | solution.py:67
  229.6 5.0 fusion.104
  234.6 4.3 fusion.109
  238.9 79.5 %all-reduce.8.cloned.1.call-done = (bf16[768,768]{1,0:T(8,128)(2,1)}, bf16[768,768]{1,0:T(8,128)(2,1)}, bf16[768,768]{1,0:T(8,128)(2,1)}) async-done(((bf16[768,768]{1,0:T(8,128)(2,1)}, bf16[768,768]{1,0:T(8,128)(2,1)}, bf16[768,768]{1,0:T(8,128)(2,1)}), (bf16[768,768]{1,0:T(8,128)(2,1)}, bf16[768,768]{1,0:T(8,128)(2,1)}, bf16[768,768]{1,0:T(8,128)(2,1)})) %all-reduce.8.cloned.1.call-update) | async-done | bytes 3538960 | tf_op jit(solution)/shard_map/psum | solution.py:87
  318.4 5.0 fusion.13
  323.4 5.9 all-to-all-start.3
  329.4 5.3 fusion.81
  334.7 3.5 fusion.14
  338.2 19.6 %all-to-all-done.3 = bf16[96,8,1280]{2,1,0:T(8,128)(2,1)} async-done(((bf16[96,8,1280]{2,1,0:T(8,128)(2,1)}), bf16[96,8,1280]{2,1,0:T(8,128)(2,1)}, u32[]{:S(2)}, u32[]{:S(2)}) %all-to-all-start.3) | async-done | bytes 1966112 | tf_op jit(solution)/shard_map/all_to_all | solution.py:74
  357.8 4.8 all-to-all-start.5
  362.6 2.1 fusion.9
  364.7 1.7 copy.123
  366.3 1.9 copy.91
  368.3 22.7 %all-to-all-done.5 = bf16[96,8,1280]{2,1,0:T(8,128)(2,1)} async-done(((bf16[96,8,1280]{2,1,0:T(8,128)(2,1)}), bf16[96,8,1280]{2,1,0:T(8,128)(2,1)}, u32[]{:S(2)}, u32[]{:S(2)}) %all-to-all-start.5) | async-done | bytes 1966112 | tf_op jit(solution)/shard_map/all_to_all | solution.py:74
  391.0 2.1 fusion.7
  393.1 1.7 copy.122
  395.3 2.5 fusion.25
  397.7 3.5 fusion.24
  401.3 2.9 collective-permute-start.1
  404.2 26.3 %collective-permute-done.1 = bf16[128,5120]{1,0:T(8,128)(2,1)} collective-permute-done((bf16[128,5120]{1,0:T(8,128)(2,1)S(1)}, bf16[128,5120]{1,0:T(8,128)(2,1)}, u32[]{:S(2)}, u32[]{:S(2)}) %collective-permute-start.1) | collective-permute-done | bytes 1310752 | tf_op jit(solution)/shard_map/ppermute | solution.py:14
  430.5 3.7 reshape.517
  434.2 2.3 convolution_convert_fusion
  436.5 2.4 copy.67
  438.8 5.3 all-to-all-start.6
  444.7 2.4 reshape.528
  448.4 5.9 fusion.62
  454.3 18.3 %all-to-all-done.6 = bf16[96,8,1280]{2,1,0:T(8,128)(2,1)} async-done(((bf16[96,8,1280]{2,1,0:T(8,128)(2,1)}), bf16[96,8,1280]{2,1,0:T(8,128)(2,1)}, u32[]{:S(2)}, u32[]{:S(2)}) %all-to-all-start.6) | async-done | bytes 1966112 | tf_op jit(solution)/shard_map/all_to_all | solution.py:67
  472.6 4.3 fusion.119
  476.9 6.1 fusion.58
  483.0 5.5 fusion.64
  488.5 33.1 %all-reduce.6.cloned.1.call-done = bf16[768,768]{1,0:T(8,128)(2,1)} async-done(((bf16[768,768]{1,0:T(8,128)(2,1)}), bf16[768,768]{1,0:T(8,128)(2,1)}) %all-reduce.6.cloned.1.call-update) | async-done | bytes 1179664 | tf_op jit(solution)/shard_map/psum | solution.py:101
  521.6 5.3 fusion.79
  526.9 3.5 fusion.15
  530.5 6.8 %all-to-all-start.7 = ((bf16[96,8,1280]{2,1,0:T(8,128)(2,1)}), bf16[96,8,1280]{2,1,0:T(8,128)(2,1)}, u32[]{:S(2)}, u32[]{:S(2)}) async-start(bf16[96,8,1280]{2,1,0:T(8,128)(2,1)} %fusion.15), calls=%async_computation.7 | async-start | bytes 3932160 | tf_op jit(solution)/shard_map/all_to_all | solution.py:74
  537.4 6.7 %fusion.18 = bf16[1,1,768,1280]{3,2,1,0:T(8,128)(2,1)} fusion(f32[768,1280]{1,0:T(8,128)} %fusion.58, bf16[96,8,1280]{2,1,0:T(8,128)(2,1)} %all-to-all-done.6, bf16[768,768]{1,0:T(8,128)(2,1)} %get-tuple-element.13, bf16[768,768]{1,0:T(8,128)(2,1)} %get-tuple-element.14), kind=kOutput, calls=%fused_computation.42 | convolution fusion | flops 1516634112 | bytes 10223616 | tf_op jit(solution)/shard_map/dot_general | solution.py:24
  544.1 3.2 fusion.17
  547.3 3.3 fusion.16
  550.6 15.2 %all-to-all-done.7 = bf16[96,8,1280]{2,1,0:T(8,128)(2,1)} async-done(((bf16[96,8,1280]{2,1,0:T(8,128)(2,1)}), bf16[96,8,1280]{2,1,0:T(8,128)(2,1)}, u32[]{:S(2)}, u32[]{:S(2)}) %all-to-all-start.7) | async-done | bytes 1966112 | tf_op jit(solution)/shard_map/all_to_all | solution.py:74
  565.7 5.9 multiply_reduce_fusion
  571.6 14.5 %psum.62 = f32[5120]{0:T(1024)S(1)} all-reduce(f32[5120]{0:T(1024)S(1)} %add.121), channel_id=1, replica_groups=mesh['dp'=4,'pipe'=4,'expert'=8] {'dp'}, use_global_device_ids=true, to_apply=%region_14.15 | all-reduce | flops 5120 | bytes 40960 | tf_op jit(solution)/shard_map/psum | solution.py:173
  586.2 24.4 %psum.63 = f32[1,5120]{1,0:T(1,128)} all-reduce(f32[1,5120]{1,0:T(1,128)S(1)} %bitcast.217), channel_id=1, replica_groups=mesh['dp'=4,'pipe'=4,'expert'=8] {'expert'}, use_global_device_ids=true, to_apply=%region_15.16 | all-reduce | flops 5120 | bytes 40960 | tf_op jit(solution)/shard_map/psum | solution.py:173
  610.6 3.4 copy.121
  614.0 2.0 copy.93
  616.1 4.0 fusion.124
  (84 shorter events, 9.2 us)
Async XLA Ops:
  7.2 108.0 %copy-start = (bf16[1,1,768,1280]{3,2,1,0:T(8,128)(2,1)S(1)}, bf16[1,1,768,1280]{3,2,1,0:T(8,128)(2,1)}, u32[]{:S(2)}) copy-start(bf16[1,1,768,1280]{3,2,1,0:T(8,128)(2,1)} %param.12) | copy-start | bytes 5898244
  7.2 2.8 copy-start.1
  7.2 108.0 %all-reduce.10.cloned.1.call-start = ((), (), s32[]{:S(2)}) async-start(), calls=%async_computation.10 | async-start | bytes 4718592 | tf_op jit(solution)/shard_map/psum | solution.py:87
  13.2 34.5 %copy-start.7 = (bf16[1,1,1280,768]{3,2,1,0:T(8,128)(2,1)S(1)}, bf16[1,1,1280,768]{3,2,1,0:T(8,128)(2,1)}, u32[]{:S(2)}) copy-start(bf16[1,1,1280,768]{3,2,1,0:T(8,128)(2,1)} %param.10) | copy-start | bytes 5898244
  47.7 2.7 copy-start.4
  47.7 2.7 copy-start.8
  155.6 32.8 %collective-permute-start = (bf16[128,5120]{1,0:T(8,128)(2,1)}, bf16[128,5120]{1,0:T(8,128)(2,1)}, u32[]{:S(2)}, u32[]{:S(2)}) collective-permute-start(bf16[128,5120]{1,0:T(8,128)(2,1)} %fusion.29), channel_id=1, source_target_pairs={{24,0},{0,8},{8,16},{16,24},{25,1},{1,9},{9,17},{17,25},{26,2},{2,... | collective-permute-start | bytes 3932168 | tf_op jit(solution)/shard_map/ppermute | solution.py:14
  163.1 26.9 %copy-start.6 = (f32[1,5120]{1,0:T(1,128)S(1)}, f32[1,5120]{1,0:T(1,128)}, u32[]{:S(2)}) copy-start(f32[1,5120]{1,0:T(1,128)} %param.9) | copy-start | bytes 61444
  163.1 33.3 %all-to-all-start.4 = ((bf16[96,8,1280]{2,1,0:T(8,128)(2,1)}), bf16[96,8,1280]{2,1,0:T(8,128)(2,1)}, u32[]{:S(2)}, u32[]{:S(2)}) async-start(bf16[96,8,1280]{2,1,0:T(8,128)(2,1)} %copy.61), calls=%async_computation.4 | async-start | bytes 3932160 | tf_op jit(solution)/shard_map/all_to_all | solution.py:67
  196.4 33.2 %all-to-all-start.2 = ((bf16[96,8,1280]{2,1,0:T(8,128)(2,1)}), bf16[96,8,1280]{2,1,0:T(8,128)(2,1)}, u32[]{:S(2)}, u32[]{:S(2)}) async-start(bf16[96,8,1280]{2,1,0:T(8,128)(2,1)} %copy.55), calls=%async_computation.2 | async-start | bytes 3932160 | tf_op jit(solution)/shard_map/all_to_all | solution.py:67
  201.2 117.2 %all-reduce.8.cloned.1.call-start = ((), (), s32[]{:S(2)}) async-start(), calls=%async_computation.9 | async-start | bytes 7077888 | tf_op jit(solution)/shard_map/psum | solution.py:87
  229.6 5.0 copy-start.9
  323.4 34.3 %all-to-all-start.3 = ((bf16[96,8,1280]{2,1,0:T(8,128)(2,1)}), bf16[96,8,1280]{2,1,0:T(8,128)(2,1)}, u32[]{:S(2)}, u32[]{:S(2)}) async-start(bf16[96,8,1280]{2,1,0:T(8,128)(2,1)} %fusion.13), calls=%async_computation.3 | async-start | bytes 3932160 | tf_op jit(solution)/shard_map/all_to_all | solution.py:74
  329.4 5.3 copy-start.10
  329.4 5.3 copy-start.16
  329.4 5.3 copy-start.18
  357.8 33.2 %all-to-all-start.5 = ((bf16[96,8,1280]{2,1,0:T(8,128)(2,1)}), bf16[96,8,1280]{2,1,0:T(8,128)(2,1)}, u32[]{:S(2)}, u32[]{:S(2)}) async-start(bf16[96,8,1280]{2,1,0:T(8,128)(2,1)} %fusion.14), calls=%async_computation.5 | async-start | bytes 3932160 | tf_op jit(solution)/shard_map/all_to_all | solution.py:74
  395.2 2.5 copy-start.2
  395.2 2.5 copy-start.3
  401.3 29.2 %collective-permute-start.1 = (bf16[128,5120]{1,0:T(8,128)(2,1)S(1)}, bf16[128,5120]{1,0:T(8,128)(2,1)}, u32[]{:S(2)}, u32[]{:S(2)}) collective-permute-start(bf16[128,5120]{1,0:T(8,128)(2,1)S(1)} %get-tuple-element.15), channel_id=1, source_target_pairs={{8,0},{16,8},{24,16},{0,24},{9,1},{17,9},{25,17},{1,25},{10,2},{18... | collective-permute-start | bytes 3932168 | tf_op jit(solution)/shard_map/ppermute | solution.py:14
  438.8 33.7 %all-to-all-start.6 = ((bf16[96,8,1280]{2,1,0:T(8,128)(2,1)}), bf16[96,8,1280]{2,1,0:T(8,128)(2,1)}, u32[]{:S(2)}, u32[]{:S(2)}) async-start(bf16[96,8,1280]{2,1,0:T(8,128)(2,1)} %copy.67), calls=%async_computation.6 | async-start | bytes 3932160 | tf_op jit(solution)/shard_map/all_to_all | solution.py:67
  444.2 77.4 %all-reduce.6.cloned.1.call-start = ((), (), s32[]{:S(2)}) async-start(), calls=%async_computation.8 | async-start | bytes 2359296 | tf_op jit(solution)/shard_map/psum | solution.py:101
  476.9 6.2 copy-start.15
  476.9 6.1 copy-start.17
  476.9 6.1 copy-start.19
  521.6 5.3 copy-start.11
  521.6 5.3 copy-start.13
  521.6 5.3 copy-start.20
  530.5 35.3 %all-to-all-start.7 = ((bf16[96,8,1280]{2,1,0:T(8,128)(2,1)}), bf16[96,8,1280]{2,1,0:T(8,128)(2,1)}, u32[]{:S(2)}, u32[]{:S(2)}) async-start(bf16[96,8,1280]{2,1,0:T(8,128)(2,1)} %fusion.15), calls=%async_computation.7 | async-start | bytes 3932160 | tf_op jit(solution)/shard_map/all_to_all | solution.py:74
  537.3 6.8 %copy-start.5 = (bf16[96,8,1280]{2,1,0:T(8,128)(2,1)S(1)}, bf16[96,8,1280]{2,1,0:T(8,128)(2,1)}, u32[]{:S(2)}) copy-start(bf16[96,8,1280]{2,1,0:T(8,128)(2,1)} %copy-done.4) | copy-start | bytes 5898244
  537.3 6.8 %copy-start.14 = (bf16[768,768]{1,0:T(8,128)(2,1)S(1)}, bf16[768,768]{1,0:T(8,128)(2,1)}, u32[]{:S(2)}) copy-start(bf16[768,768]{1,0:T(8,128)(2,1)} %get-tuple-element.14) | copy-start | bytes 3538948
  537.3 6.8 %copy-start.21 = (bf16[768,768]{1,0:T(8,128)(2,1)S(1)}, bf16[768,768]{1,0:T(8,128)(2,1)}, u32[]{:S(2)}) copy-start(bf16[768,768]{1,0:T(8,128)(2,1)} %all-reduce.6.cloned.1.call-done) | copy-start | bytes 3538948
  537.3 6.8 %copy-start.22 = (f32[1280,768]{1,0:T(8,128)S(1)}, f32[1280,768]{1,0:T(8,128)}, u32[]{:S(2)}) copy-start(f32[1280,768]{1,0:T(8,128)} %fusion.62) | copy-start | bytes 11796484
  544.1 3.2 copy-start.12
  544.1 3.2 copy-start.23
Sparse Core Ops, SparseCore 0:
  53.3 61.8 all-reduce.9
  239.0 79.3 all-reduce.7
  477.0 44.5 all-reduce.5
